TPU v7x, 512 devices: a whole 4x8x8 slice. The times are simulated.
512 devices in a mesh: tile: 128 (over z, y, core), fft: 4 (over x).
Axes of the slice: x: 4, y: 8, z: 8, core: 2. Of those that a mesh axis runs over, the one named last changes fastest.
Arguments:
- residual_sky_tiles: float32 [4096, 128, 128], P(('tile', 'fft')), may hold values from -6 to 6
- cover: int32 [128, 256], replicated, may hold values from -1 to 4095, as said below
- beam_width: float32 [128], replicated, may hold values from 1 to 2
- transfer: bfloat16 [2048, 2048], P('fft'), may hold values from 0.049804688 to 1
Outputs:
- gradient: float32 [4096, 128, 128], P(('tile', 'fft'))
Inputs may be any that keep to these rules, and one draw needn't show every extreme that they name: `cover`: pointing p covers the 16 x 16 block of sky map tiles with its corner at some tile row and column; entry i * 16 + j names the tile at sky map row r = corner row + i and column c = corner column + j, or is -1 where r is outside 0 to 63 or c outside 0 to 63. Tile (r, c) has id ((c mod 16) + 16 * (r mod 32)) * 8 + (r div 32) * 4 + c div 16. Every pointing names at least one tile; pointing 0 has its corner at row 0, column 0. No pointing names more than 1 tiles whose ids share the same value of id div 8, and pointing 0 names exactly 1 such tiles.
All inputs are finite; a program needn't handle non-finite values.
Results may differ from a plain program's by a relative error of at most 0.01.
Values may be sent and summed in bfloat16 or wider, within the bound.
A program may use at most 64 MiB of HBM per device.

v0:
```python
import math

import jax
import jax.numpy as jnp
from jax import lax
from jax.sharding import PartitionSpec as P

PT = 16
FA = 64
RH = 2


def make_tables(first_len, second):
    total_len = first_len * second
    first_ids = jnp.arange(first_len, dtype=jnp.int32)
    second_ids = jnp.arange(second, dtype=jnp.int32)
    sample_ids = second_ids[:, None] + second * first_ids[None, :]
    prod_one = sample_ids[:, :, None] * first_ids[None, None, :] % total_len
    angle_one = 2.0 * math.pi / total_len * prod_one.astype(jnp.float32)
    table_one = jnp.stack([jnp.cos(angle_one), -jnp.sin(angle_one)], axis=2).astype(jnp.bfloat16)
    prod_two = second_ids[:, None] * second_ids[None, :] % second
    angle_two = 2.0 * math.pi / second * prod_two.astype(jnp.float32)
    cos_two = jnp.cos(angle_two)
    sin_two = jnp.sin(angle_two)
    table_two = jnp.stack([cos_two + sin_two, sin_two - cos_two], axis=0).astype(jnp.bfloat16)
    return (table_one, table_two)


def hartley(field_in, tables_all):
    table_one, table_two = tables_all
    second = table_one.shape[0]
    first_len = table_one.shape[1]
    columns = field_in.shape[1]
    shaped = field_in.reshape(first_len, second, columns)
    section_two = jnp.einsum(
        "mra,rmtk->rtka", shaped, table_one, preferred_element_type=jnp.float32
    ).astype(jnp.bfloat16)
    result = jnp.einsum("rtka,trj->jka", section_two, table_two, preferred_element_type=jnp.float32)
    return result.reshape(first_len * second, columns)


def hartley_last(field_in, tables_all):
    table_one, table_two = tables_all
    second = table_one.shape[0]
    first_len = table_one.shape[1]
    rows = field_in.shape[0]
    shaped = field_in.reshape(rows, first_len, second)
    section_two = jnp.einsum(
        "amr,rmtk->rtka", shaped, table_one, preferred_element_type=jnp.float32
    ).astype(jnp.bfloat16)
    result = jnp.einsum("rtka,trj->ajk", section_two, table_two, preferred_element_type=jnp.float32)
    return result.reshape(rows, first_len * second)


def shards(residual_sky_tiles, cover, beam_width, transfer):
    tiles_held = residual_sky_tiles.shape[0]
    tile_side = residual_sky_tiles.shape[1]
    groups = lax.axis_size("tile")
    slab_count = lax.axis_size("fft")
    pointing_tiles = cover.shape[1]
    image_side = tile_side * PT
    slab_rows = image_side // slab_count
    quarter_section = PT // slab_count
    band_rows = groups * slab_count // PT
    slot_count = max(1, min(PT // band_rows, RH))
    group_index = lax.axis_index("tile")
    slab_index = lax.axis_index("fft")
    myself = group_index * slab_count + slab_index
    tables_all = make_tables(FA, image_side // FA)
    holder_all = jnp.where(cover >= 0, cover // tiles_held, -1)
    local_all = jnp.where(cover >= 0, cover % tiles_held, -1)
    mine = holder_all == myself
    order_all = jnp.cumsum(mine.astype(jnp.int32), axis=1) - 1
    slot_ids = jnp.arange(slot_count, dtype=jnp.int32)
    held_ids = jnp.arange(tiles_held, dtype=jnp.int32)
    selected_entry = (mine[:, None, :] & (order_all[:, None, :] == slot_ids[None, :, None])).astype(
        jnp.bfloat16
    )
    found_position = (local_all[:, :, None] == held_ids[None, None, :]).astype(jnp.bfloat16)
    selector = jnp.einsum(
        "qlf,qft->qlt", selected_entry, found_position, preferred_element_type=jnp.float32
    ).astype(jnp.bfloat16)
    sending = jnp.einsum(
        "gck,kxy->gcxy",
        selector,
        residual_sky_tiles.astype(jnp.bfloat16),
        preferred_element_type=jnp.float32,
    ).astype(jnp.bfloat16)
    arrived = lax.all_to_all(sending, "tile", split_axis=0, concat_axis=0, tiled=True)
    own_cover = lax.dynamic_index_in_dim(cover, group_index, 0, keepdims=False)
    own_holder = jnp.where(own_cover >= 0, own_cover // tiles_held, -1)
    positions = jnp.arange(pointing_tiles, dtype=jnp.int32)
    earlier = (own_holder[None, :] == own_holder[:, None]) & (
        positions[None, :] < positions[:, None]
    )
    rank_own = jnp.sum(earlier.astype(jnp.int32), axis=1)
    slot_of = own_holder // slab_count * slot_count + rank_own
    column_of = positions % PT
    col_phase = jnp.max(
        jnp.where(own_cover >= 0, (own_holder % slab_count - column_of) % slab_count, 0)
    )
    row_ids = jnp.arange(PT, dtype=jnp.int32)
    quarter_ids = jnp.arange(quarter_section, dtype=jnp.int32)
    my_cols = slab_count * quarter_ids + (slab_index - col_phase) % slab_count
    my_pos = row_ids[:, None] * PT + my_cols[None, :]
    my_live = (own_cover[my_pos] >= 0).reshape(-1)
    my_slot = jnp.where(my_live, slot_of[my_pos].reshape(-1), 0)
    flat_arrived = arrived.reshape(groups * slot_count, tile_side, tile_side)
    tile_placement = jnp.take(flat_arrived, my_slot, axis=0)
    tile_placement = jnp.where(my_live[:, None, None], tile_placement, jnp.zeros((), jnp.bfloat16))
    tile_placement = tile_placement.reshape(PT, quarter_section, tile_side, tile_side)
    slab_ids = jnp.arange(slab_count, dtype=jnp.int32)
    source_of = (slab_ids + col_phase) % slab_count
    target_of = (slab_ids - col_phase) % slab_count
    outgoing = jnp.transpose(tile_placement, (1, 0, 2, 3))
    incoming = lax.all_to_all(outgoing, "fft", split_axis=0, concat_axis=0, tiled=True)
    ordered = jnp.take(incoming, source_of, axis=0)
    image_rows = jnp.transpose(ordered, (1, 2, 0, 3)).reshape(
        image_side, quarter_section * tile_side
    )
    tile_cols = slab_count * slab_index + quarter_ids
    fwhm_frac = lax.dynamic_index_in_dim(beam_width, group_index, 0, keepdims=False)
    center = (image_side - 1) / 2.0
    spread_sq = (fwhm_frac * image_side) ** 2
    row_coord = jnp.arange(image_side, dtype=jnp.float32) - center
    column_pixel_span = (
        tile_cols[:, None] * tile_side + jnp.arange(tile_side, dtype=jnp.int32)[None, :]
    )
    col_coord = column_pixel_span.reshape(-1).astype(jnp.float32) - center
    row_factor = jnp.exp(-4.0 * math.log(2.0) * row_coord * row_coord / spread_sq)
    col_factor = jnp.exp(-4.0 * math.log(2.0) * col_coord * col_coord / spread_sq)
    weighted = (row_factor[:, None] * col_factor[None, :] * image_rows.astype(jnp.float32)).astype(
        jnp.bfloat16
    )
    rowwise = hartley(weighted, tables_all).astype(jnp.bfloat16)
    turned = lax.all_to_all(rowwise, "fft", split_axis=0, concat_axis=1, tiled=True)
    spectrum = hartley_last(turned, tables_all).astype(jnp.bfloat16)
    filtered = (transfer.astype(jnp.float32) * spectrum.astype(jnp.float32)).astype(jnp.bfloat16)
    back_cols = hartley_last(filtered, tables_all).astype(jnp.bfloat16)
    leaving = back_cols.reshape(slab_rows, slab_count, quarter_section * tile_side)
    returned = lax.all_to_all(leaving, "fft", split_axis=1, concat_axis=0, tiled=True)
    returned = returned.reshape(image_side, quarter_section * tile_side)
    smeared = hartley(returned, tables_all)
    contribution = (
        row_factor[:, None] * col_factor[None, :] * smeared / (image_side * image_side)
    ).astype(jnp.bfloat16)
    pieces = jnp.transpose(
        contribution.reshape(PT, tile_side, quarter_section, tile_side), (2, 0, 1, 3)
    )
    pieces = jnp.take(pieces, target_of, axis=0)
    gathered_back = lax.all_to_all(pieces, "fft", split_axis=0, concat_axis=0, tiled=True)
    own_tiles = jnp.transpose(gathered_back, (1, 0, 2, 3))
    own_tiles = own_tiles.reshape(PT * quarter_section, tile_side, tile_side)
    all_slots = jnp.arange(groups * slot_count, dtype=jnp.int32)
    list_ids = jnp.arange(PT * quarter_section, dtype=jnp.int32)
    slot_match = (my_slot[None, :] == all_slots[:, None]) & my_live[None, :]
    slot_live = jnp.any(slot_match, axis=1)
    slot_source = jnp.sum(jnp.where(slot_match, list_ids[None, :], 0), axis=1)
    returning = jnp.take(own_tiles, slot_source, axis=0)
    returning = jnp.where(slot_live[:, None, None], returning, jnp.zeros((), jnp.bfloat16))
    returning = returning.reshape(groups, slot_count, tile_side, tile_side)
    back_arrived = lax.all_to_all(returning, "tile", split_axis=0, concat_axis=0, tiled=True)
    return jnp.einsum("gck,gcxy->kxy", selector, back_arrived, preferred_element_type=jnp.float32)


def solution(mesh):
    placed = (P(("tile", "fft"), None, None), P(), P(), P("fft", None))
    return jax.shard_map(
        shards,
        mesh=mesh,
        in_specs=placed,
        out_specs=P(("tile", "fft"), None, None),
        check_vma=False,
    )
```

profile of v0, /device:TPU:33, one launch (start us, length us, event | category | flops | bytes accessed | tf_op | source)
XLA Modules:
  0.0 462.2 jit_solution(14400180133558399171)
XLA Ops:
  0.0 1.0 copy.67
  1.2 0.1 fusion.45
  1.4 0.1 add_compare_fusion
  1.8 0.2 select_reduce_fusion
  2.1 1.1 convert_element_type.135
  3.2 1.3 convert_bitcast_fusion.2
  4.5 4.7 %copy.79 = bf16[128,1,128,128]{3,2,1,0:T(8,128)(2,1)} copy(bf16[128,1,128,128]{3,0,2,1:T(8,128)(2,1)S(1)} %convert_bitcast_fusion.2) | data formatting | bytes 8388608 | tf_op jit(solution)/shard_map/convert_element_type | solution.py:88
  9.1 17.8 %all-to-all-start = ((bf16[128,1,128,128]{3,2,1,0:T(8,128)(2,1)}), bf16[128,1,128,128]{3,2,1,0:T(8,128)(2,1)}, u32[]{:S(2)}, u32[]{:S(2)}) async-start(bf16[128,1,128,128]{3,2,1,0:T(8,128)(2,1)} %copy.79), calls=%async_computation | async-start | bytes 8388608 | tf_op jit(solution)/shard_map/all_to_all | solution.py:89
  26.9 0.7 compare_select_fusion.2
  27.7 0.7 fusion.77
  29.2 0.8 gather_fusion
  30.0 0.2 convert_reduce_fusion
  30.2 0.8 gather_fusion.1
  31.5 97.7 %all-to-all-done = bf16[128,1,128,128]{3,2,1,0:T(8,128)(2,1)} async-done(((bf16[128,1,128,128]{3,2,1,0:T(8,128)(2,1)}), bf16[128,1,128,128]{3,2,1,0:T(8,128)(2,1)}, u32[]{:S(2)}, u32[]{:S(2)}) %all-to-all-start) | async-done | bytes 4194336 | tf_op jit(solution)/shard_map/all_to_all | solution.py:89
  129.2 3.1 gather_fusion.2
  132.4 1.6 fusion.27
  134.0 4.6 all-to-all-start.1
  138.6 0.6 dynamic_slice.9
  140.5 0.7 compare_select_fusion.4
  141.1 0.7 compare_and_fusion.2
  142.1 4.4 cosine_convert_fusion
  146.5 18.0 %all-to-all-done.1 = bf16[4,16,128,128]{3,2,1,0:T(8,128)(2,1)} async-done(((bf16[4,16,128,128]{3,2,1,0:T(8,128)(2,1)}), bf16[4,16,128,128]{3,2,1,0:T(8,128)(2,1)}, u32[]{:S(2)}, u32[]{:S(2)}) %all-to-all-start.1) | async-done | bytes 2097184 | tf_op jit(solution)/shard_map/all_to_all | solution.py:116
  164.5 2.5 gather_fusion.4
  167.1 0.3 convert_bitcast_fusion.1
  167.4 4.7 %copy.81 = f32[16,128,4,128]{3,2,1,0:T(4,128)} copy(f32[16,128,4,128]{3,1,0,2:T(8,128)S(1)} %convert_bitcast_fusion.1) | data formatting | bytes 8388608 | tf_op jit(solution)/shard_map/convert_element_type | solution.py:132
  172.2 5.5 %reshape.491 = f32[64,32,512]{2,1,0:T(8,128)} reshape(f32[16,128,4,128]{3,2,1,0:T(4,128)} %copy.81) | data formatting | bytes 8388608 | tf_op jit(solution)/shard_map/convert_element_type | solution.py:132
  177.6 2.6 fusion.19
  180.3 2.9 convolution_convert_fusion.3
  183.2 5.1 %bitcast_convert_fusion.2 = bf16[32,64,512]{2,0,1:T(8,128)(2,1)S(1)} fusion(bf16[32,2,64,512]{3,2,1,0:T(8,128)(2,1)S(1)} %convolution_convert_fusion.3, bf16[1,32,32]{1,2,0:T(8,128)(2,1)S(1)} %get-tuple-element.16, bf16[1,32,32]{1,2,0:T(8,128)(2,1)S(1)} %get-tuple-element.17), kind=kOutput, calls=%fused_computation.15 | convolution fusion | flops 135274496 | bytes 6295552 | tf_op jit(solution)/shard_map/rtka,trj->jka/dot_general | solution.py:38
  188.3 2.5 copy.84
  190.8 3.6 all-to-all-start.2
  194.4 3.9 copy.75
  198.3 21.0 %all-to-all-done.2 = bf16[4,512,512]{2,1,0:T(8,128)(2,1)S(1)} async-done(((bf16[4,512,512]{2,1,0:T(8,128)(2,1)}), bf16[4,512,512]{2,1,0:T(8,128)(2,1)S(1)}, u32[]{:S(2)}, u32[]{:S(2)}) %all-to-all-start.2) | async-done | bytes 2097184 | tf_op jit(solution)/shard_map/all_to_all | solution.py:136
  219.3 1.3 copy-done.2
  220.6 3.0 copy.85
  223.6 2.8 convolution_convert_fusion.2
  226.4 5.2 %convert_bitcast_fusion = f32[512,32,64]{0,1,2:T(8,128)S(1)} fusion(bf16[32,2,64,512]{3,2,1,0:T(8,128)(2,1)S(1)} %convolution_convert_fusion.2, bf16[1,32,32]{1,2,0:T(8,128)(2,1)S(1)} %get-tuple-element.16, bf16[1,32,32]{1,2,0:T(8,128)(2,1)S(1)} %get-tuple-element.17), kind=kOutput, calls=%fused_computation.28 | convolution fusion | flops 136323072 | bytes 8392704 | tf_op jit(solution)/shard_map/rtka,trj->ajk/dot_general | solution.py:51
  231.6 2.4 copy.88
  234.1 0.8 fusion.4
  234.8 3.3 convolution_convert_fusion.1
  238.1 5.1 %fusion.21 = bf16[512,32,64]{0,1,2:T(8,128)(2,1)S(1)} fusion(bf16[32,2,64,512]{3,2,1,0:T(8,128)(2,1)S(1)} %convolution_convert_fusion.1, bf16[1,32,32]{1,2,0:T(8,128)(2,1)S(1)} %get-tuple-element.16, bf16[1,32,32]{1,2,0:T(8,128)(2,1)S(1)} %get-tuple-element.17), kind=kOutput, calls=%fused_computation.39 | convolution fusion | flops 135274496 | bytes 6295552 | tf_op jit(solution)/shard_map/rtka,trj->ajk/dot_general | solution.py:51
  243.3 2.5 copy.91
  245.8 3.8 all-to-all-start.3
  249.6 0.7 compare_select_fusion.3
  250.2 0.7 compare_and_fusion.1
  251.0 22.5 %all-to-all-done.3 = bf16[512,4,512]{0,2,1:T(8,128)(2,1)S(1)} async-done(((bf16[512,4,512]{0,2,1:T(8,128)(2,1)}), bf16[512,4,512]{0,2,1:T(8,128)(2,1)S(1)}, u32[]{:S(2)}, u32[]{:S(2)}) %all-to-all-start.3) | async-done | bytes 2097184 | tf_op jit(solution)/shard_map/all_to_all | solution.py:141
  273.5 1.3 copy-done.1
  274.8 2.8 copy.92
  277.6 2.8 convolution_convert_fusion
  280.4 5.2 %fusion.16 = f32[32,64,512]{2,0,1:T(8,128)S(1)} fusion(bf16[32,2,64,512]{3,2,1,0:T(8,128)(2,1)S(1)} %convolution_convert_fusion, bf16[1,32,32]{1,2,0:T(8,128)(2,1)S(1)} %get-tuple-element.16, bf16[1,32,32]{1,2,0:T(8,128)(2,1)S(1)} %get-tuple-element.17), kind=kOutput, calls=%fused_computation.36 | convolution fusion | flops 134225920 | bytes 8392704 | tf_op jit(solution)/shard_map/rtka,trj->jka/dot_general | solution.py:38
  285.6 4.4 copy.95
  290.0 5.4 %reshape.487 = f32[16,128,4,128]{3,2,1,0:T(4,128)} reshape(f32[32,64,512]{2,1,0:T(8,128)} %copy.95) | data formatting | bytes 8388608 | tf_op jit(solution)/shard_map/reshape | solution.py:39
  295.5 3.0 fusion.20
  298.4 2.2 gather_fusion.5
  300.6 3.2 broadcast_select_fusion
  303.8 3.6 all-to-all-start.4
  307.7 22.8 %all-to-all-done.4 = bf16[4,16,128,128]{3,2,1,0:T(8,128)(2,1)S(1)} async-done(((bf16[4,16,128,128]{3,2,1,0:T(8,128)(2,1)}), bf16[4,16,128,128]{3,2,1,0:T(8,128)(2,1)S(1)}, u32[]{:S(2)}, u32[]{:S(2)}) %all-to-all-start.4) | async-done | bytes 2097184 | tf_op jit(solution)/shard_map/all_to_all | solution.py:151
  330.4 1.3 copy-done
  331.8 1.7 copy.97
  333.5 3.0 gather_fusion.3
  336.5 2.7 fusion.3
  339.3 119.5 %all_to_all.48 = bf16[128,1,128,128]{3,2,1,0:T(8,128)(2,1)S(1)} all-to-all(bf16[128,1,128,128]{3,2,1,0:T(8,128)(2,1)S(1)} %fusion.3), channel_id=1, replica_groups=mesh['tile'=128,'fft'=4] {'tile'}, dimensions={0} | all-to-all | bytes 8388608 | tf_op jit(solution)/shard_map/all_to_all | solution.py:162
  458.8 2.3 fusion
  461.1 0.9 copy.100
  (48 shorter events, 1.7 us)
Async XLA Ops:
  9.1 120.1 %all-to-all-start = ((bf16[128,1,128,128]{3,2,1,0:T(8,128)(2,1)}), bf16[128,1,128,128]{3,2,1,0:T(8,128)(2,1)}, u32[]{:S(2)}, u32[]{:S(2)}) async-start(bf16[128,1,128,128]{3,2,1,0:T(8,128)(2,1)} %copy.79), calls=%async_computation | async-start | bytes 8388608 | tf_op jit(solution)/shard_map/all_to_all | solution.py:89
  132.4 6.3 %copy-start.4 = (f32[128]{0:T(128)S(1)}, f32[128]{0:T(128)}, u32[]{:S(2)}) copy-start(f32[128]{0:T(128)} %param.8) | copy-start | bytes 1540
  134.0 30.5 %all-to-all-start.1 = ((bf16[4,16,128,128]{3,2,1,0:T(8,128)(2,1)}), bf16[4,16,128,128]{3,2,1,0:T(8,128)(2,1)}, u32[]{:S(2)}, u32[]{:S(2)}) async-start(bf16[4,16,128,128]{3,2,1,0:T(8,128)(2,1)} %fusion.27), calls=%async_computation.1 | async-start | bytes 4194304 | tf_op jit(solution)/shard_map/all_to_all | solution.py:116
  190.8 28.5 %all-to-all-start.2 = ((bf16[4,512,512]{2,1,0:T(8,128)(2,1)}), bf16[4,512,512]{2,1,0:T(8,128)(2,1)S(1)}, u32[]{:S(2)}, u32[]{:S(2)}) async-start(bf16[4,512,512]{2,1,0:T(8,128)(2,1)} %bitcast.105), calls=%async_computation.2 | async-start | bytes 4194304 | tf_op jit(solution)/shard_map/all_to_all | solution.py:136
  219.3 1.3 copy-start.2
  231.6 2.4 copy-start.3
  245.8 27.7 %all-to-all-start.3 = ((bf16[512,4,512]{0,2,1:T(8,128)(2,1)}), bf16[512,4,512]{0,2,1:T(8,128)(2,1)S(1)}, u32[]{:S(2)}, u32[]{:S(2)}) async-start(bf16[512,4,512]{0,2,1:T(8,128)(2,1)} %bitcast.103), calls=%async_computation.3 | async-start | bytes 4194304 | tf_op jit(solution)/shard_map/all_to_all | solution.py:141
  273.5 1.3 copy-start.1
  303.8 26.6 %all-to-all-start.4 = ((bf16[4,16,128,128]{3,2,1,0:T(8,128)(2,1)}), bf16[4,16,128,128]{3,2,1,0:T(8,128)(2,1)S(1)}, u32[]{:S(2)}, u32[]{:S(2)}) async-start(bf16[4,16,128,128]{3,2,1,0:T(8,128)(2,1)} %broadcast_select_fusion), calls=%async_computation.4 | async-start | bytes 4194304 | tf_op jit(solution)/shard_map/all_to_all | solution.py:151
  330.4 1.3 copy-start
where the time goes:
time: 470 us; the launch traced here: 462 us
  waiting for transfers between devices  182 us (39%)
  blocking collectives  119 us (25%)
  local copies, waits for them, and re-layouts  63.3 us (13%)
  matrix products  36 us (8%)
  starting transfers between devices  33.4 us (7%)
  other arithmetic  25.4 us (5%)
    all_to_all x1, blocking collectives, shards(): lax.all_to_all(returning, 'tile', split_axis=0, concat_axis=0, tiled=True)  119 us
    all_to_all x1, waiting for transfers between devices, shards(): lax.all_to_all(sending, 'tile', split_axis=0, concat_axis=0, tiled=True)  97.7 us
    all_to_all x1, waiting for transfers between devices, shards(): lax.all_to_all(pieces, 'fft', split_axis=0, concat_axis=0, tiled=True)  22.8 us
    all_to_all x1, waiting for transfers between devices, shards(): lax.all_to_all(leaving, 'fft', split_axis=1, concat_axis=0, tiled=True)  22.5 us
    all_to_all x1, waiting for transfers between devices, shards(): lax.all_to_all(rowwise, 'fft', split_axis=0, concat_axis=1, tiled=True)  21 us
    all_to_all x1, waiting for transfers between devices, shards(): lax.all_to_all(outgoing, 'fft', split_axis=0, concat_axis=0, tiled=True)  18 us
    all_to_all x1, starting transfers between devices, shards(): lax.all_to_all(sending, 'tile', split_axis=0, concat_axis=0, tiled=True)  17.8 us
    dot_general x2, matrix products, hartley(): jnp.einsum('rtka,trj->jka', section_two, table_two, preferred_element_typ...  10.3 us
  transfers between devices with their start and end apart: 5, of which 5 were waited for; matrix products, arithmetic and copies ran while one was open for 3% of the time, Pallas kernels for 0%

commit v1 on v0

v1 whole, which is shorter than its diff:
```python
import math

import jax
import jax.numpy as jnp
import ml_dtypes
import numpy as np
from jax import lax
from jax.experimental import pallas as pl
from jax.experimental.pallas import tpu as pltpu
from jax.sharding import Mesh
from jax.sharding import PartitionSpec as P

PT = 16
ROWS = 64
COLS = 64
SIDE = 128
L = 2048
SLAB = 512
HALF = 256
HELD = 8
RELAY_X = True
RELAY_Y = True
MESH = pl.DeviceIdType.MESH
BF = jnp.bfloat16
F32 = jnp.float32


def hartley_matrix(length):
    ids = np.arange(length, dtype=np.int64)
    angle = 2.0 * np.pi / length * ((ids[:, None] * ids[None, :]) % length)
    return (np.cos(angle) + np.sin(angle)).astype(np.float32).astype(ml_dtypes.bfloat16)


def corners(cover, tiles_held):
    live = cover >= 0
    holder = cover // tiles_held
    local = cover % tiles_held
    rows = holder // PT + 32 * (local // 4)
    cols = holder % PT + PT * (local % 4)
    position = jnp.arange(PT * PT, dtype=jnp.int32)
    row_at = jnp.max(jnp.where(live, rows - position // PT, -1000), axis=1)
    col_at = jnp.max(jnp.where(live, cols - position % PT, -1000), axis=1)
    return row_at, col_at


def wait_bytes(ref, sem):
    pltpu.make_async_copy(ref, ref, sem).wait()


def kernel(
    row_at, col_at, width, sky, t_hbm, tcol_hbm, transfer_hbm, out,
    tv, tcol, trv, row_beam, col_beam, sel, p0, p1, p2, p3, send, img0, img1, w, rowsend, turned, a, spec, filt,
    backsend, ret, csend, grecv, part, rss, rsr, xrel, yrel, crel,
    load_sem, ag_send, ag_recv, y_send, y_recv, x_send, x_recv, b_send, b_recv, c_send, c_recv, rs_send, rs_recv,
    xr_recv, xf_send, yr_recv, yf_send, cr_recv, cf_send,
):
    z, y = lax.axis_index("z"), lax.axis_index("y")
    core, x = lax.axis_index("core"), lax.axis_index("fft")
    me16 = y * 2 + core
    yhi = lax.div(y, 2)
    odd = lax.rem(y, 2)
    far_y = lax.rem(y + 4, 8)
    col_class = x + 4 * core + 8 * odd
    up = {"z": lax.rem(z + 1, 8)}
    down = {"z": lax.rem(z + 7, 8)}
    pairs = [p0, p1, p2, p3]
    images = [img0, img1]
    order_in = (2, 1, 3, 0)
    order_out = (0, 1, 3, 2)

    def remote(src, dst, s_sem, r_sem, where):
        return pltpu.make_async_remote_copy(
            src_ref=src, dst_ref=dst, send_sem=s_sem, recv_sem=r_sem, device_id=where, device_id_type=MESH
        )

    def tile_index(delta, d):
        row, col = row_at[z * 16 + d], col_at[z * 16 + d]
        sky_row = row + lax.rem(yhi + 4 * lax.rem(z + delta, 4) - row + 1024, 16)
        sky_col = col + lax.rem(col_class - col + 1024, 16)
        live = (sky_row >= 0) & (sky_row < ROWS) & (sky_col >= 0) & (sky_col < COLS)
        which = lax.div(lax.rem(lax.div(sky_row, 4) - z - delta + 64, 8), 4)
        return jnp.where(live, which * 8 + lax.div(sky_row, 32) * 4 + lax.div(sky_col, 16), 16)

    load_t = pltpu.make_async_copy(t_hbm, tv, load_sem.at[0])
    load_tr = pltpu.make_async_copy(transfer_hbm, trv, load_sem.at[1])
    load_tcol = pltpu.make_async_copy(tcol_hbm, tcol, load_sem.at[2])

    barrier = pltpu.get_barrier_semaphore()
    pl.semaphore_signal(barrier, inc=1, device_id=up, device_id_type=MESH)
    pl.semaphore_signal(barrier, inc=1, device_id=down, device_id_type=MESH)

    @pl.loop(1, 16)
    def _(step):
        d = lax.rem(me16 + step, 16)
        pl.semaphore_signal(
            barrier, inc=1, device_id={"y": lax.div(d, 2), "core": lax.rem(d, 2)}, device_id_type=MESH
        )

    for step in range(1, 4):
        pl.semaphore_signal(barrier, inc=1, device_id={"fft": lax.rem(x + step, 4)}, device_id_type=MESH)
    load_t.start()
    load_tr.start()
    load_tcol.start()
    p0[0:8] = sky[...].astype(BF)
    for pair in pairs:
        pair[16] = jnp.zeros((SIDE, SIDE), BF)
    pl.semaphore_wait(barrier, 20)

    ring = [
        [(p0.at[0:8], p1.at[0:8], down), (p0.at[0:8], p3.at[8:16], up)],
        [(p1.at[0:8], p2.at[0:8], down), (p3.at[8:16], p2.at[8:16], up)],
        [(p2.at[0:8], p3.at[0:8], down), (p2.at[8:16], p1.at[8:16], up)],
        [(p3.at[0:4], p0.at[8:12], down), (p1.at[12:16], p0.at[12:16], up)],
    ]

    def ring_copies(step):
        return [
            remote(src, dst, ag_send.at[2 * step + way], ag_recv.at[2 * step + way], to)
            for way, (src, dst, to) in enumerate(ring[step])
        ]

    def stage(delta):
        pair = pairs[delta]

        @pl.loop(0, 16)
        def _(d):
            send[delta, d] = pair[tile_index(delta, d)]

    def push(delta, half):
        m = lax.rem(z + delta, 4)
        dst = images[half].at[m * 4 + yhi, core]
        r_sem = y_recv.at[half, delta]
        if RELAY_Y:
            for way in range(2):
                to = {"y": lax.rem(y + 1 + 6 * way, 8)}
                remote(
                    send.at[delta, far_y * 2 + way], yrel.at[delta, way], y_send.at[delta], yr_recv.at[delta, way], to
                ).start()

        @pl.loop(1, 16)
        def _(step):
            d = lax.rem(me16 + step, 16)
            to = {"y": lax.div(d, 2), "core": lax.rem(d, 2)}
            direct = remote(send.at[delta, d], dst, y_send.at[delta], r_sem, to)
            if RELAY_Y:
                pl.when(lax.div(d, 2) != far_y)(direct.start)
            else:
                direct.start()

        pltpu.make_async_copy(send.at[delta, me16], dst, r_sem).start()

    def forward_tile(delta, half):
        m = lax.rem(z + delta, 4)
        for way in range(2):
            source = lax.rem(y + 7 - 6 * way, 8)
            to = {"y": lax.rem(y + 3 + 2 * way, 8), "core": way}
            dst = images[half].at[m * 4 + lax.div(source, 2), core]
            wait_bytes(yrel.at[delta, way], yr_recv.at[delta, way])
            remote(yrel.at[delta, way], dst, yf_send, y_recv.at[half, delta], to).start()

    started = []
    for step in range(4):
        now = ring_copies(step)
        for copy in now:
            copy.start()
        started += now
        ready = {2: (2,), 3: (1, 3)}.get(step, ())
        for delta in ready:
            stage(delta)

            @pl.when(odd == 0)
            def _():
                push(delta, 0)

        for copy in now:
            copy.wait_recv()
    stage(0)

    @pl.when(odd == 0)
    def _():
        push(0, 0)

    center = (L - 1) / 2.0
    point = z * 16 + me16
    row_turn = lax.rem(row_at[point] + 1024, 16)
    col_turn = lax.rem(col_at[point] + 1024, 16)
    span = jnp.full((SIDE, SIDE), width[point], F32) * L
    rate = (-4.0 * math.log(2.0)) / (span * span)

    @pl.loop(0, 16)
    def _(i):
        coord = (i * SIDE + lax.broadcasted_iota(jnp.int32, (SIDE, SIDE), 0)).astype(F32) - center
        row_beam[i] = jnp.exp(rate * (coord * coord))

    for s in range(4):
        block = lax.rem(x + 4 * s + 16 - col_turn, 16)
        coord = (block * SIDE + lax.broadcasted_iota(jnp.int32, (8, SIDE), 1)).astype(F32) - center
        col_beam[:, s * SIDE : (s + 1) * SIDE] = jnp.exp(rate[0:8] * (coord * coord))

    @pl.loop(0, 4)
    def _(delta):
        lane = lax.broadcasted_iota(jnp.int32, (8, 256), 1)

        def place(p, acc):
            inside = (lane >= 16 * p) & (lane < 16 * p + 16)
            return jnp.where(inside, tile_index(delta, p) * 16 + lane - 16 * p, acc)

        target = lax.fori_loop(0, 16, place, jnp.zeros((8, 256), jnp.int32))
        row = lax.broadcasted_iota(jnp.int32, (256, 256), 0)
        sel[delta] = jnp.where(row == target[0:1], 1.0, 0.0).astype(BF)

    load_t.wait()
    load_tr.wait()
    load_tcol.wait()

    def wait_chunk(half, delta):
        wait_bytes(images[half].at[0:4], y_recv.at[half, delta])

    def weigh(half):
        image = images[half]

        @pl.loop(0, 16)
        def _(i):
            rc = lax.rem(i + row_turn, 16)
            rows = pl.ds(i * SIDE, SIDE)
            for c in range(2):
                s = c + 2 * half
                beam = row_beam[i] * col_beam[0:1, s * SIDE : (s + 1) * SIDE]
                tile = image[rc, c].astype(F32)
                w[half, rows, c * SIDE : (c + 1) * SIDE] = (beam * tile).astype(BF)

    def deliver(blocks, home, s_sem, r_sem, r_sems, stops, rel, xd):
        if RELAY_X:

            @pl.when((rel == 1) | (rel == 3))
            def _():
                for c in range(2):
                    remote(blocks[c], home[c], s_sem, r_sem, {"fft": xd}).start()

            @pl.when(rel == 2)
            def _():
                for c in range(2):
                    to = {"fft": lax.rem(x + 1 + 2 * c, 4)}
                    remote(blocks[c], stops[c], s_sem, r_sems.at[c], to).start()

        else:

            @pl.when(rel != 0)
            def _():
                for c in range(2):
                    remote(blocks[c], home[c], s_sem, r_sem, {"fft": xd}).start()

        @pl.when(rel == 0)
        def _():
            for c in range(2):
                pltpu.make_async_copy(blocks[c], home[c], r_sem).start()

    def pass_blocks(stops, homes, f_sem, r_sem, r_sems):
        if RELAY_X:
            for c in range(2):
                wait_bytes(stops[c], r_sems.at[c])
                remote(stops[c], homes[c], f_sem, r_sem, {"fft": lax.rem(x + 1 + 2 * c, 4)}).start()

    def row_transform(half):
        stops = [xrel.at[0, half, c] for c in range(2)]

        @pl.loop(0, 4)
        def _(t):
            rel = lax.rem(2 + t + lax.div(t, 2) + 2 * lax.div(t, 3), 4)
            xd = lax.rem(x + rel, 4)
            slab = jnp.dot(tv[pl.ds(xd * 4, 4)].reshape(SLAB, L), w[half], preferred_element_type=F32).astype(BF)
            for c in range(2):
                rowsend[half, xd, c] = slab[:, c * SIDE : (c + 1) * SIDE]
            blocks = [rowsend.at[half, xd, c] for c in range(2)]
            home = [turned.at[x + 4 * c + 8 * half] for c in range(2)]
            deliver(blocks, home, x_send.at[half], x_recv.at[half], xr_recv.at[0, half], stops, rel, xd)

        homes = [turned.at[lax.rem(x + 3 - 2 * c, 4) + 4 * c + 8 * half] for c in range(2)]
        pass_blocks(stops, homes, xf_send.at[0], x_recv.at[half], xr_recv.at[0, half])

    for at, delta in enumerate(order_in):
        if at == 3:

            @pl.when(odd == 1)
            def _():
                push(order_in[0], 1)
                push(order_in[1], 1)

        if RELAY_Y:

            @pl.when(odd == 1)
            def _():
                forward_tile(delta, 0)

        wait_chunk(0, delta)

    @pl.when(odd == 1)
    def _():
        push(order_in[2], 1)
        push(order_in[3], 1)

    weigh(0)
    row_transform(0)
    if RELAY_Y:

        @pl.when(odd == 0)
        def _():
            for delta in order_in:
                forward_tile(delta, 1)

    for delta in order_in:
        wait_chunk(1, delta)
    weigh(1)
    row_transform(1)

    for half in range(2):
        wait_bytes(turned.at[8 * half : 8 * half + 8], x_recv.at[half])
        for k in range(8):
            a[half, :, k * SIDE : (k + 1) * SIDE] = turned[8 * half + k]
        places = [lax.rem(8 * half + k + 16 - col_turn, 16) for k in range(8)]
        for n in range(4):
            cols = slice(n * SLAB, (n + 1) * SLAB)
            rhs = jnp.concatenate([tv[j, :, cols] for j in places], axis=0)
            total = jnp.dot(a[half], rhs, preferred_element_type=F32)
            if half == 0:
                spec[:, cols] = total
            else:
                spectrum = (spec[:, cols] + total).astype(BF)
                filt[:, cols] = (trv[:, cols].astype(F32) * spectrum.astype(F32)).astype(BF)

    for half in range(2):
        stops = [xrel.at[1, half, c] for c in range(2)]

        @pl.loop(0, 4)
        def _(t):
            rel = lax.rem(2 + t + lax.div(t, 2) + 2 * lax.div(t, 3), 4)
            xd = lax.rem(x + rel, 4)
            picked = [tcol[lax.rem(xd + 4 * c + 8 * half + 16 - col_turn, 16)] for c in range(2)]
            back = jnp.dot(filt[...], jnp.concatenate(picked, axis=1), preferred_element_type=F32).astype(BF)
            for c in range(2):
                backsend[half, xd, c] = back[:, c * SIDE : (c + 1) * SIDE]
            blocks = [backsend.at[half, xd, c] for c in range(2)]
            home = [ret.at[half, c, x] for c in range(2)]
            deliver(blocks, home, b_send.at[half], b_recv.at[half], xr_recv.at[1, half], stops, rel, xd)

        homes = [ret.at[half, c, lax.rem(x + 3 - 2 * c, 4)] for c in range(2)]
        pass_blocks(stops, homes, xf_send.at[1], b_recv.at[half], xr_recv.at[1, half])

    def forward_back(delta):
        for way in range(2):
            source = lax.rem(y + 7 - 6 * way, 8)
            to = {"y": lax.rem(y + 3 + 2 * way, 8), "core": way}
            wait_bytes(crel.at[delta, way], cr_recv.at[delta, way])
            remote(crel.at[delta, way], grecv.at[delta, source * 2 + core], cf_send, c_recv.at[delta], to).start()

    for turn in range(8):
        half, delta = turn // 4, order_out[turn % 4]
        if turn % 4 == 0:
            wait_bytes(ret.at[half], b_recv.at[half])
        m = lax.rem(z + delta, 4)
        places = [lax.rem(4 * m + yh + 16 - row_turn, 16) for yh in range(4)]
        lhs = jnp.concatenate([tv[i] for i in places], axis=0)
        rhs = jnp.concatenate([ret[half, c].reshape(L, SIDE) for c in range(2)], axis=1)
        smeared = jnp.dot(lhs, rhs, preferred_element_type=F32)
        for yh in range(4):
            rows = row_beam[places[yh]]
            for c in range(2):
                s = c + 2 * half
                beam = rows * col_beam[0:1, s * SIDE : (s + 1) * SIDE]
                tile = smeared[yh * SIDE : (yh + 1) * SIDE, c * SIDE : (c + 1) * SIDE]
                csend[half, delta, yh, c] = (beam * tile * (1.0 / (L * L))).astype(BF)

        @pl.loop(0, 8)
        def _(step):
            yh = lax.rem(yhi + lax.div(step, 2) + 2, 4)
            c = lax.rem(step, 2)
            yd = 2 * yh + half
            mine = jnp.logical_and(yd == y, c == core)
            far = yd == far_y
            src = csend.at[half, delta, yh, c]
            home = grecv.at[delta, me16]
            if RELAY_Y:

                @pl.when(far)
                def _():
                    to = {"y": lax.rem(y + 1 + 6 * c, 8)}
                    remote(src, crel.at[delta, c], c_send.at[half], cr_recv.at[delta, c], to).start()

                direct = jnp.logical_not(jnp.logical_or(mine, far))
            else:
                direct = jnp.logical_not(mine)

            @pl.when(direct)
            def _():
                remote(src, home, c_send.at[half], c_recv.at[delta], {"y": yd, "core": c}).start()

            @pl.when(mine)
            def _():
                pltpu.make_async_copy(src, home, c_recv.at[delta]).start()

        if RELAY_Y and 2 <= turn <= 5:

            @pl.when(odd == 1)
            def _():
                forward_back(order_out[turn - 2])

        if RELAY_Y and turn >= 6:

            @pl.when(odd == 0)
            def _():
                forward_back(order_out[turn - 6])

    if RELAY_Y:

        @pl.when(odd == 0)
        def _():
            forward_back(order_out[2])
            forward_back(order_out[3])

    def add_up(delta):
        wait_bytes(grecv.at[delta], c_recv.at[delta])

        @pl.loop(0, 8)
        def _(b):
            rows = pl.ds(b * 16, 16)
            stack = grecv[delta, :, rows, :].reshape(256, SIDE)
            total = jnp.dot(sel[delta], stack, preferred_element_type=F32)
            part[delta, :, rows, :] = total.reshape(16, 16, SIDE)

    def pass_on(step, way, value, tiles):
        k = 2 * step + way
        rss[k, tiles] = value.astype(BF)
        copy = remote(rss.at[k, tiles], rsr.at[k, tiles], rs_send.at[k], rs_recv.at[k], (up, down)[way])
        copy.start()
        return copy

    low, high, every = slice(0, 4), slice(4, 8), slice(0, 8)
    add_up(0)
    first = [pass_on(0, 0, part[0, 8:12], low), pass_on(0, 1, part[0, 12:16], high)]
    add_up(3)
    add_up(1)
    first[0].wait_recv()
    part[3, 0:4] = part[3, 0:4] + rsr[0, 0:4].astype(F32)
    second = [pass_on(1, 0, part[3, 0:8], every)]
    first[1].wait_recv()
    part[1, 12:16] = part[1, 12:16] + rsr[1, 4:8].astype(F32)
    second.append(pass_on(1, 1, part[1, 8:16], every))
    add_up(2)
    second[0].wait_recv()
    third = [pass_on(2, 0, part[2, 0:8] + rsr[2].astype(F32), every)]
    second[1].wait_recv()
    third.append(pass_on(2, 1, part[2, 8:16] + rsr[3].astype(F32), every))
    third[0].wait_recv()
    last = [pass_on(3, 0, part[1, 0:8] + rsr[4].astype(F32), every)]
    third[1].wait_recv()
    last.append(pass_on(3, 1, part[3, 8:16] + rsr[5].astype(F32), every))

    for copy in started:
        copy.wait_send()
    for delta in range(4):
        wait_bytes(send.at[delta, 0:15], y_send.at[delta])
    for half in range(2):
        wait_bytes(rowsend.at[half, 0:3], x_send.at[half])
        wait_bytes(backsend.at[half, 0:3], b_send.at[half])

        @pl.when(odd == half)
        def _():
            wait_bytes(csend.at[half, :, 0:3], c_send.at[half])
            wait_bytes(csend.at[half, :, 3, 0], c_send.at[half])

        @pl.when(odd != half)
        def _():
            wait_bytes(csend.at[half], c_send.at[half])

    if RELAY_X:
        for way in range(2):
            wait_bytes(xrel.at[way], xf_send.at[way])
    if RELAY_Y:
        wait_bytes(yrel, yf_send)
        wait_bytes(crel, cf_send)
    last[0].wait_recv()
    last[1].wait_recv()
    out[...] = part[0, 0:8] + rsr[6].astype(F32) + rsr[7].astype(F32)
    for copy in first + second + third + last:
        copy.wait_send()


def make_shards(table):
    by_rows = table.reshape(PT, SIDE, L)
    by_cols = np.ascontiguousarray(table.reshape(L, PT, SIDE).transpose(1, 0, 2))

    def shards(residual_sky_tiles, cover, beam_width, transfer):
        row_at, col_at = corners(cover, HELD)
        vmem = pl.BlockSpec(memory_space=pltpu.VMEM)
        smem = pl.BlockSpec(memory_space=pltpu.SMEM)
        anywhere = pl.BlockSpec(memory_space=pl.ANY)
        tile = (SIDE, SIDE)
        dma = pltpu.SemaphoreType.DMA
        scratch = [
            pltpu.VMEM((PT, SIDE, L), BF),
            pltpu.VMEM((PT, L, SIDE), BF),
            pltpu.VMEM((SLAB, L), BF),
            pltpu.VMEM((PT,) + tile, F32),
            pltpu.VMEM((8, SLAB), F32),
            pltpu.VMEM((4, 256, 256), BF),
            pltpu.VMEM((17,) + tile, BF),
            pltpu.VMEM((17,) + tile, BF),
            pltpu.VMEM((17,) + tile, BF),
            pltpu.VMEM((17,) + tile, BF),
            pltpu.VMEM((4, 16) + tile, BF),
            pltpu.VMEM((16, 2) + tile, BF),
            pltpu.VMEM((16, 2) + tile, BF),
            pltpu.VMEM((2, L, HALF), BF),
            pltpu.VMEM((2, 4, 2, SLAB, SIDE), BF),
            pltpu.VMEM((16, SLAB, SIDE), BF),
            pltpu.VMEM((2, SLAB, L // 2), BF),
            pltpu.VMEM((SLAB, L), F32),
            pltpu.VMEM((SLAB, L), BF),
            pltpu.VMEM((2, 4, 2, SLAB, SIDE), BF),
            pltpu.VMEM((2, 2, 4, SLAB, SIDE), BF),
            pltpu.VMEM((2, 4, 4, 2) + tile, BF),
            pltpu.VMEM((4, 16) + tile, BF),
            pltpu.VMEM((4, 16) + tile, F32),
            pltpu.VMEM((8, 8) + tile, BF),
            pltpu.VMEM((8, 8) + tile, BF),
            pltpu.VMEM((2, 2, 2, SLAB, SIDE), BF),
            pltpu.VMEM((4, 2) + tile, BF),
            pltpu.VMEM((4, 2) + tile, BF),
            dma((3,)),
            dma((8,)),
            dma((8,)),
            dma((4,)),
            dma((2, 4)),
            dma((2,)),
            dma((2,)),
            dma((2,)),
            dma((2,)),
            dma((2,)),
            dma((4,)),
            dma((8,)),
            dma((8,)),
            dma((2, 2, 2)),
            dma((2,)),
            dma((4, 2)),
            pltpu.SemaphoreType.DMA,
            dma((4, 2)),
            pltpu.SemaphoreType.DMA,
        ]
        return pl.pallas_call(
            kernel,
            out_shape=jax.ShapeDtypeStruct((HELD,) + tile, F32),
            in_specs=[smem, smem, smem, vmem, anywhere, anywhere, anywhere],
            out_specs=vmem,
            scratch_shapes=scratch,
            compiler_params=pltpu.CompilerParams(
                collective_id=0, has_side_effects=True, vmem_limit_bytes=63 * 1024 * 1024
            ),
            cost_estimate=pl.CostEstimate(flops=4 * 2 * L * L * SLAB, bytes_accessed=20 * 2**20, transcendentals=0),
        )(row_at, col_at, beam_width, residual_sky_tiles, jnp.asarray(by_rows), jnp.asarray(by_cols), transfer)

    return shards


def solution(mesh):
    split = Mesh(mesh.devices.reshape(8, 8, 2, 4), ("z", "y", "core", "fft"))
    over_all = P(("z", "y", "core", "fft"), None, None)
    return jax.shard_map(
        make_shards(hartley_matrix(L)),
        mesh=split,
        in_specs=(over_all, P(), P(), P("fft", None)),
        out_specs=over_all,
        check_vma=False,
    )
```

time: 470 us -> 203 us (0.43)
  the two profiles are of different devices: /device:TPU:33 before, /device:TPU:10 now
where the time goes in v1:
time: 203 us
  Pallas kernels  199 us (98%)
    pallas_call x1, Pallas kernels, shards(): pl.pallas_call(kernel, out_shape=jax.ShapeDtypeStruct((HELD,) + tile, F32...  199 us

profile of v1, /device:TPU:10, one launch (start us, length us, event | category | flops | bytes accessed | tf_op | source)
XLA Modules:
  0.0 202.5 jit_solution(17898218359798714912)
XLA Ops:
  0.0 2.0 fusion.8
  2.0 198.7 %shard_map.64 = f32[8,128,128]{2,1,0:T(8,128)} custom-call(s32[128]{0:T(128)} %get-tuple-element.6.row_at, s32[128]{0:T(128)} %get-tuple-element.5.col_at, f32[128]{0:T(128)} %width.1, f32[8,128,128]{2,1,0:T(8,128)} %sky.1, bf16[16,128,2048]{2,1,0:T(8,128)(2,1)} %constant.98.clone.t_hbm, bf16[16,2048,128]{2,1,0:T(8,128)(2,1)} %constant.99.clone.tcol_hbm, ...), custom_call_target="tpu_custom_call" | custom-call | flops 17179869184 | bytes 20971520 | tf_op jit(solution)/shard_map/pallas_call | solution.py:549
  200.6 1.9 copy.8
  (1 shorter events, 0.0 us)

commit v2 on v1

v2 whole, which is shorter than its diff:
```python
import math

import jax
import jax.numpy as jnp
import ml_dtypes
import numpy as np
from jax import lax
from jax.experimental import pallas as pl
from jax.experimental.pallas import tpu as pltpu
from jax.sharding import Mesh
from jax.sharding import PartitionSpec as P

PT = 16
ROWS = 64
COLS = 64
SIDE = 128
L = 2048
SLAB = 512
HALF = 256
HELD = 8
SUBS = 4
MESH = pl.DeviceIdType.MESH
BF = jnp.bfloat16
F32 = jnp.float32


def hartley_matrix(length):
    ids = np.arange(length, dtype=np.int64)
    angle = 2.0 * np.pi / length * ((ids[:, None] * ids[None, :]) % length)
    return (np.cos(angle) + np.sin(angle)).astype(np.float32).astype(ml_dtypes.bfloat16)


def corners(cover, tiles_held):
    live = cover >= 0
    holder = cover // tiles_held
    local = cover % tiles_held
    rows = holder // PT + 32 * (local // 4)
    cols = holder % PT + PT * (local % 4)
    position = jnp.arange(PT * PT, dtype=jnp.int32)
    row_at = jnp.max(jnp.where(live, rows - position // PT, -1000), axis=1)
    col_at = jnp.max(jnp.where(live, cols - position % PT, -1000), axis=1)
    return row_at, col_at


def wait_bytes(ref, sem):
    pltpu.make_async_copy(ref, ref, sem).wait()


def kernel(
    row_at, col_at, width, sky, t_hbm, tcol_hbm, transfer_hbm, out,
    tv, tcol, trv, row_beam, col_beam, sel, p0, p1, p2, p3, send, img0, img1, img2, img3, w, rowsend, turned, a, spec, filt,
    backsend, ret, csend, grecv, part, rss, rsr, xrel,
    load_sem, ag_send, ag_recv, y_send, y_recv, x_send, x_recv, b_send, b_recv, c_send, c_recv, rs_send, rs_recv,
    xr_recv, xf_send,
):
    z, y = lax.axis_index("z"), lax.axis_index("y")
    core, x = lax.axis_index("core"), lax.axis_index("fft")
    me16 = y * 2 + core
    yhi = lax.div(y, 2)
    odd = lax.rem(y, 2)
    phase = core + 2 * odd
    col_class = x + 4 * core + 8 * odd
    up = {"z": lax.rem(z + 1, 8)}
    down = {"z": lax.rem(z + 7, 8)}
    pairs = [p0, p1, p2, p3]
    images = [img0, img1, img2, img3]
    order_in = (2, 1, 3, 0)
    order_out = (0, 1, 3, 2)

    def remote(src, dst, s_sem, r_sem, where):
        return pltpu.make_async_remote_copy(
            src_ref=src, dst_ref=dst, send_sem=s_sem, recv_sem=r_sem, device_id=where, device_id_type=MESH
        )

    def tile_index(delta, d):
        row, col = row_at[z * 16 + d], col_at[z * 16 + d]
        sky_row = row + lax.rem(yhi + 4 * lax.rem(z + delta, 4) - row + 1024, 16)
        sky_col = col + lax.rem(col_class - col + 1024, 16)
        live = (sky_row >= 0) & (sky_row < ROWS) & (sky_col >= 0) & (sky_col < COLS)
        which = lax.div(lax.rem(lax.div(sky_row, 4) - z - delta + 64, 8), 4)
        return jnp.where(live, which * 8 + lax.div(sky_row, 32) * 4 + lax.div(sky_col, 16), 16)

    load_t = pltpu.make_async_copy(t_hbm, tv, load_sem.at[0])
    load_tr = pltpu.make_async_copy(transfer_hbm, trv, load_sem.at[1])
    load_tcol = pltpu.make_async_copy(tcol_hbm, tcol, load_sem.at[2])

    barrier = pltpu.get_barrier_semaphore()
    pl.semaphore_signal(barrier, inc=1, device_id=up, device_id_type=MESH)
    pl.semaphore_signal(barrier, inc=1, device_id=down, device_id_type=MESH)

    @pl.loop(1, 16)
    def _(step):
        d = lax.rem(me16 + step, 16)
        pl.semaphore_signal(
            barrier, inc=1, device_id={"y": lax.div(d, 2), "core": lax.rem(d, 2)}, device_id_type=MESH
        )

    for step in range(1, 4):
        pl.semaphore_signal(barrier, inc=1, device_id={"fft": lax.rem(x + step, 4)}, device_id_type=MESH)
    load_t.start()
    load_tr.start()
    load_tcol.start()
    p0[0:8] = sky[...].astype(BF)
    for pair in pairs:
        pair[16] = jnp.zeros((SIDE, SIDE), BF)
    pl.semaphore_wait(barrier, 20)

    ring = [
        [(p0.at[0:8], p1.at[0:8], down), (p0.at[0:8], p3.at[8:16], up)],
        [(p1.at[0:8], p2.at[0:8], down), (p3.at[8:16], p2.at[8:16], up)],
        [(p2.at[0:8], p3.at[0:8], down), (p2.at[8:16], p1.at[8:16], up)],
        [(p3.at[0:4], p0.at[8:12], down), (p1.at[12:16], p0.at[12:16], up)],
    ]

    def ring_copy(step, way, sub):
        src, dst, to = ring[step][way]
        part_of = pl.ds(2 * sub if step < 3 else 2 * (sub - 2 * way), 2)
        k = (step * 2 + way) * SUBS + sub
        return remote(src.at[part_of], dst.at[part_of], ag_send.at[k], ag_recv.at[k], to)

    def stage(delta):
        pair = pairs[delta]

        @pl.loop(0, 16)
        def _(d):
            send[delta, d] = pair[tile_index(delta, d)]

    def push(delta, s):
        m = lax.rem(z + delta, 4)
        dst = images[s].at[m * 4 + yhi]
        r_sem = y_recv.at[s, delta]

        @pl.loop(1, 16)
        def _(step):
            d = lax.rem(me16 + step, 16)
            to = {"y": lax.div(d, 2), "core": lax.rem(d, 2)}
            remote(send.at[delta, d], dst, y_send.at[delta], r_sem, to).start()

        pltpu.make_async_copy(send.at[delta, me16], dst, r_sem).start()

    started = []
    for step in range(4):
        now = []
        for sub in range(SUBS):
            for way in range(2):
                if step > 0:
                    ring_copy(step - 1, way, sub).wait_recv()
                if step < 3 or sub // 2 == way:
                    copy = ring_copy(step, way, sub)
                    copy.start()
                    now.append(copy)
        started += now
        for delta in {2: (2,), 3: (1, 3)}.get(step, ()):
            stage(delta)

            @pl.when(phase == 0)
            def _():
                push(delta, 0)

    for copy in now:
        copy.wait_recv()
    stage(0)

    @pl.when(phase == 0)
    def _():
        push(0, 0)

    center = (L - 1) / 2.0
    point = z * 16 + me16
    row_turn = lax.rem(row_at[point] + 1024, 16)
    col_turn = lax.rem(col_at[point] + 1024, 16)
    span = jnp.full((SIDE, SIDE), width[point], F32) * L
    rate = (-4.0 * math.log(2.0)) / (span * span)

    @pl.loop(0, 16)
    def _(i):
        coord = (i * SIDE + lax.broadcasted_iota(jnp.int32, (SIDE, SIDE), 0)).astype(F32) - center
        row_beam[i] = jnp.exp(rate * (coord * coord))

    for s in range(4):
        block = lax.rem(x + 4 * s + 16 - col_turn, 16)
        coord = (block * SIDE + lax.broadcasted_iota(jnp.int32, (8, SIDE), 1)).astype(F32) - center
        col_beam[:, s * SIDE : (s + 1) * SIDE] = jnp.exp(rate[0:8] * (coord * coord))

    @pl.loop(0, 4)
    def _(delta):
        lane = lax.broadcasted_iota(jnp.int32, (8, 256), 1)

        def place(p, acc):
            inside = (lane >= 16 * p) & (lane < 16 * p + 16)
            return jnp.where(inside, tile_index(delta, p) * 16 + lane - 16 * p, acc)

        target = lax.fori_loop(0, 16, place, jnp.zeros((8, 256), jnp.int32))
        row = lax.broadcasted_iota(jnp.int32, (256, 256), 0)
        sel[delta] = jnp.where(row == target[0:1], 1.0, 0.0).astype(BF)

    load_t.wait()
    load_tr.wait()
    load_tcol.wait()

    def wait_chunk(s, delta):
        wait_bytes(images[s].at[0:4], y_recv.at[s, delta])

    def weigh(s):
        image = images[s]

        @pl.loop(0, 16)
        def _(i):
            rc = lax.rem(i + row_turn, 16)
            beam = row_beam[i] * col_beam[0:1, s * SIDE : (s + 1) * SIDE]
            w[s, pl.ds(i * SIDE, SIDE), :] = (beam * image[rc].astype(F32)).astype(BF)

    halves = [slice(0, HALF), slice(HALF, SLAB)]

    def deliver(block, home, stops, s_sem, r_sem, r_sems, rel, xd):
        @pl.when((rel == 1) | (rel == 3))
        def _():
            remote(block, home, s_sem, r_sem, {"fft": xd}).start()

        @pl.when(rel == 2)
        def _():
            for c in range(2):
                to = {"fft": lax.rem(x + 1 + 2 * c, 4)}
                remote(block.at[halves[c]], stops[c], s_sem, r_sems.at[c], to).start()

        @pl.when(rel == 0)
        def _():
            pltpu.make_async_copy(block, home, r_sem).start()

    def pass_blocks(stops, homes, f_sem, r_sem, r_sems):
        for c in range(2):
            wait_bytes(stops[c], r_sems.at[c])
            home = homes[c].at[halves[c]]
            remote(stops[c], home, f_sem, r_sem, {"fft": lax.rem(x + 1 + 2 * c, 4)}).start()

    sources = [lax.rem(x + 3 - 2 * c, 4) for c in range(2)]

    def row_transform(s):
        stops = [xrel.at[0, s, c] for c in range(2)]

        @pl.loop(0, 4)
        def _(t):
            rel = lax.rem(2 + t + lax.div(t, 2) + 2 * lax.div(t, 3), 4)
            xd = lax.rem(x + rel, 4)
            slab = jnp.dot(tv[pl.ds(xd * 4, 4)].reshape(SLAB, L), w[s], preferred_element_type=F32)
            rowsend[s, xd] = slab.astype(BF)
            deliver(
                rowsend.at[s, xd], turned.at[x + 4 * s], stops, x_send.at[s], x_recv.at[s], xr_recv.at[0, s], rel, xd
            )

        homes = [turned.at[source + 4 * s] for source in sources]
        pass_blocks(stops, homes, xf_send.at[0], x_recv.at[s], xr_recv.at[0, s])

    def add_spectrum(s):
        wait_bytes(turned.at[4 * s : 4 * s + 4], x_recv.at[s])
        for k in range(4):
            a[s, :, k * SIDE : (k + 1) * SIDE] = turned[4 * s + k]
        places = [lax.rem(4 * s + k + 16 - col_turn, 16) for k in range(4)]
        for n in range(4):
            cols = slice(n * SLAB, (n + 1) * SLAB)
            rhs = jnp.concatenate([tv[j, :, cols] for j in places], axis=0)
            total = jnp.dot(a[s], rhs, preferred_element_type=F32)
            if s > 0:
                total = spec[:, cols] + total
            if s < 3:
                spec[:, cols] = total
            else:
                filt[:, cols] = (trv[:, cols].astype(F32) * total.astype(BF).astype(F32)).astype(BF)

    for s in range(4):
        for at, delta in enumerate(order_in):
            if at == 3 and s < 3:

                @pl.when(phase == s + 1)
                def _():
                    push(order_in[0], s + 1)
                    push(order_in[1], s + 1)

            wait_chunk(s, delta)
        if s < 3:

            @pl.when(phase == s + 1)
            def _():
                push(order_in[2], s + 1)
                push(order_in[3], s + 1)

        weigh(s)
        row_transform(s)
        if s > 0:
            add_spectrum(s - 1)
    add_spectrum(3)

    def back_transform(s):
        stops = [xrel.at[1, s, c] for c in range(2)]

        @pl.loop(0, 4)
        def _(t):
            rel = lax.rem(2 + t + lax.div(t, 2) + 2 * lax.div(t, 3), 4)
            xd = lax.rem(x + rel, 4)
            picked = tcol[lax.rem(xd + 4 * s + 16 - col_turn, 16)]
            backsend[s, xd] = jnp.dot(filt[...], picked, preferred_element_type=F32).astype(BF)
            deliver(
                backsend.at[s, xd], ret.at[s, x], stops, b_send.at[s], b_recv.at[s], xr_recv.at[1, s], rel, xd
            )

        homes = [ret.at[s, source] for source in sources]
        pass_blocks(stops, homes, xf_send.at[1], b_recv.at[s], xr_recv.at[1, s])

    def give_back(s):
        wait_bytes(ret.at[s], b_recv.at[s])

        @pl.loop(0, 4)
        def _(turn):
            delta = turn + lax.div(turn, 2) * (5 - 2 * turn)
            m = lax.rem(z + delta, 4)
            places = [lax.rem(4 * m + yh + 16 - row_turn, 16) for yh in range(4)]
            lhs = jnp.concatenate([tv[i] for i in places], axis=0)
            smeared = jnp.dot(lhs, ret[s].reshape(L, SIDE), preferred_element_type=F32)
            for yh in range(4):
                beam = row_beam[places[yh]] * col_beam[0:1, s * SIDE : (s + 1) * SIDE]
                tile = smeared[yh * SIDE : (yh + 1) * SIDE]
                csend[s, delta, yh] = (beam * tile * (1.0 / (L * L))).astype(BF)

            @pl.loop(0, 4)
            def _(step):
                yh = lax.rem(yhi + step + 2, 4)
                yd = 2 * yh + s // 2
                mine = jnp.logical_and(yd == y, core == s % 2)
                src = csend.at[s, delta, yh]
                home = grecv.at[delta, me16]

                @pl.when(jnp.logical_not(mine))
                def _():
                    remote(src, home, c_send.at[s], c_recv.at[delta], {"y": yd, "core": s % 2}).start()

                @pl.when(mine)
                def _():
                    pltpu.make_async_copy(src, home, c_recv.at[delta]).start()

    back_transform(0)
    back_transform(1)
    give_back(0)
    back_transform(2)
    give_back(1)
    back_transform(3)
    give_back(2)
    give_back(3)

    def add_up(delta):
        wait_bytes(grecv.at[delta], c_recv.at[delta])

        @pl.loop(0, 8)
        def _(b):
            rows = pl.ds(b * 16, 16)
            stack = grecv[delta, :, rows, :].reshape(256, SIDE)
            total = jnp.dot(sel[delta], stack, preferred_element_type=F32)
            part[delta, :, rows, :] = total.reshape(16, 16, SIDE)

    def pass_on(step, way, sub, value):
        tiles = slice(2 * sub, 2 * sub + 2)
        k = 2 * step + way
        rss[k, tiles] = value.astype(BF)
        sem = k * SUBS + sub
        copy = remote(rss.at[k, tiles], rsr.at[k, tiles], rs_send.at[sem], rs_recv.at[sem], (up, down)[way])
        copy.start()
        return copy

    def landed(copies, step, way, sub):
        copies[step, way, sub].wait_recv()
        return rsr[2 * step + way, 2 * sub : 2 * sub + 2].astype(F32)

    passed = {}
    classes = [((0, 8), (0, 8)), ((3, 0), (1, 8)), ((2, 0), (2, 8)), ((1, 0), (3, 8))]
    for step in range(4):
        for delta in ((0,), (3, 1), (2,), ())[step]:
            add_up(delta)
        for sub in range(SUBS):
            for way in range(2):
                if step == 0 and sub // 2 != way:
                    continue
                delta, at = classes[step][way]
                value = part[delta, at + 2 * sub : at + 2 * sub + 2]
                if (step - 1, way, sub) in passed:
                    value = value + landed(passed, step - 1, way, sub)
                passed[step, way, sub] = pass_on(step, way, sub, value)

    for copy in started:
        copy.wait_send()
    for delta in range(4):
        wait_bytes(send.at[delta, 0:15], y_send.at[delta])
    for s in range(4):
        wait_bytes(rowsend.at[s, 0:3], x_send.at[s])
        wait_bytes(backsend.at[s, 0:3], b_send.at[s])

        @pl.when(phase == s)
        def _():
            wait_bytes(csend.at[s, :, 0:3], c_send.at[s])

        @pl.when(phase != s)
        def _():
            wait_bytes(csend.at[s], c_send.at[s])

    for way in range(2):
        wait_bytes(xrel.at[way], xf_send.at[way])
    for sub in range(SUBS):
        tiles = slice(2 * sub, 2 * sub + 2)
        out[tiles] = part[0, tiles] + landed(passed, 3, 0, sub) + landed(passed, 3, 1, sub)
    for copy in passed.values():
        copy.wait_send()


def make_shards(table):
    by_rows = table.reshape(PT, SIDE, L)
    by_cols = np.ascontiguousarray(table.reshape(L, PT, SIDE).transpose(1, 0, 2))

    def shards(residual_sky_tiles, cover, beam_width, transfer):
        row_at, col_at = corners(cover, HELD)
        vmem = pl.BlockSpec(memory_space=pltpu.VMEM)
        smem = pl.BlockSpec(memory_space=pltpu.SMEM)
        anywhere = pl.BlockSpec(memory_space=pl.ANY)
        tile = (SIDE, SIDE)
        dma = pltpu.SemaphoreType.DMA
        scratch = [
            pltpu.VMEM((PT, SIDE, L), BF),
            pltpu.VMEM((PT, L, SIDE), BF),
            pltpu.VMEM((SLAB, L), BF),
            pltpu.VMEM((PT,) + tile, F32),
            pltpu.VMEM((8, SLAB), F32),
            pltpu.VMEM((4, 256, 256), BF),
            pltpu.VMEM((17,) + tile, BF),
            pltpu.VMEM((17,) + tile, BF),
            pltpu.VMEM((17,) + tile, BF),
            pltpu.VMEM((17,) + tile, BF),
            pltpu.VMEM((4, 16) + tile, BF),
            pltpu.VMEM((16,) + tile, BF),
            pltpu.VMEM((16,) + tile, BF),
            pltpu.VMEM((16,) + tile, BF),
            pltpu.VMEM((16,) + tile, BF),
            pltpu.VMEM((4, L, SIDE), BF),
            pltpu.VMEM((4, 4, SLAB, SIDE), BF),
            pltpu.VMEM((16, SLAB, SIDE), BF),
            pltpu.VMEM((4, SLAB, SLAB), BF),
            pltpu.VMEM((SLAB, L), F32),
            pltpu.VMEM((SLAB, L), BF),
            pltpu.VMEM((4, 4, SLAB, SIDE), BF),
            pltpu.VMEM((4, 4, SLAB, SIDE), BF),
            pltpu.VMEM((4, 4, 4) + tile, BF),
            pltpu.VMEM((4, 16) + tile, BF),
            pltpu.VMEM((4, 16) + tile, F32),
            pltpu.VMEM((8, 8) + tile, BF),
            pltpu.VMEM((8, 8) + tile, BF),
            pltpu.VMEM((2, 4, 2, HALF, SIDE), BF),
            dma((3,)),
            dma((8 * SUBS,)),
            dma((8 * SUBS,)),
            dma((4,)),
            dma((4, 4)),
            dma((4,)),
            dma((4,)),
            dma((4,)),
            dma((4,)),
            dma((4,)),
            dma((4,)),
            dma((8 * SUBS,)),
            dma((8 * SUBS,)),
            dma((2, 4, 2)),
            dma((2,)),
        ]
        return pl.pallas_call(
            kernel,
            out_shape=jax.ShapeDtypeStruct((HELD,) + tile, F32),
            in_specs=[smem, smem, smem, vmem, anywhere, anywhere, anywhere],
            out_specs=vmem,
            scratch_shapes=scratch,
            compiler_params=pltpu.CompilerParams(
                collective_id=0, has_side_effects=True, vmem_limit_bytes=63 * 1024 * 1024
            ),
            cost_estimate=pl.CostEstimate(flops=4 * 2 * L * L * SLAB, bytes_accessed=20 * 2**20, transcendentals=0),
        )(row_at, col_at, beam_width, residual_sky_tiles, jnp.asarray(by_rows), jnp.asarray(by_cols), transfer)

    return shards


def solution(mesh):
    split = Mesh(mesh.devices.reshape(8, 8, 2, 4), ("z", "y", "core", "fft"))
    over_all = P(("z", "y", "core", "fft"), None, None)
    return jax.shard_map(
        make_shards(hartley_matrix(L)),
        mesh=split,
        in_specs=(over_all, P(), P(), P("fft", None)),
        out_specs=over_all,
        check_vma=False,
    )
```

time: 203 us -> 197 us (0.970)
  the two profiles are of different devices: /device:TPU:10 before, /device:TPU:9 now
where the time goes in v2:
time: 197 us; the launch traced here: 196 us
  Pallas kernels  192 us (97%)
  other arithmetic  1.97 us (1%)
    pallas_call x1, Pallas kernels, shards(): pl.pallas_call(kernel, out_shape=jax.ShapeDtypeStruct((HELD,) + tile, F32...  192 us

profile of v2, /device:TPU:9, one launch (start us, length us, event | category | flops | bytes accessed | tf_op | source)
XLA Modules:
  0.0 196.3 jit_solution(3485426224251008065)
XLA Ops:
  0.0 2.0 fusion.8
  2.0 192.5 %shard_map.64 = f32[8,128,128]{2,1,0:T(8,128)} custom-call(s32[128]{0:T(128)} %get-tuple-element.6.row_at, s32[128]{0:T(128)} %get-tuple-element.5.col_at, f32[128]{0:T(128)} %width.1, f32[8,128,128]{2,1,0:T(8,128)} %sky.1, bf16[16,128,2048]{2,1,0:T(8,128)(2,1)} %constant.98.clone.t_hbm, bf16[16,2048,128]{2,1,0:T(8,128)(2,1)} %constant.99.clone.tcol_hbm, ...), custom_call_target="tpu_custom_call" | custom-call | flops 17179869184 | bytes 20971520 | tf_op jit(solution)/shard_map/pallas_call | solution.py:469
  194.5 1.9 copy.8
  (1 shorter events, 0.0 us)

commit v3 on v2

--- a/solution.py
+++ b/solution.py
@@ -130,11 +130,16 @@
         dst = images[s].at[m * 4 + yhi]
         r_sem = y_recv.at[s, delta]
 
-        @pl.loop(1, 16)
-        def _(step):
-            d = lax.rem(me16 + step, 16)
-            to = {"y": lax.div(d, 2), "core": lax.rem(d, 2)}
-            remote(send.at[delta, d], dst, y_send.at[delta], r_sem, to).start()
+        @pl.loop(0, 8)
+        def _(k):
+            offset = 4 + (1 - 2 * lax.rem(k, 2)) * lax.div(k + 1, 2)
+            yd = lax.rem(y + offset, 8)
+            for c in range(2):
+                d = 2 * yd + c
+
+                @pl.when(d != me16)
+                def _():
+                    remote(send.at[delta, d], dst, y_send.at[delta], r_sem, {"y": yd, "core": c}).start()
 
         pltpu.make_async_copy(send.at[delta, me16], dst, r_sem).start()
 
@@ -156,6 +161,12 @@
             @pl.when(phase == 0)
             def _():
                 push(delta, 0)
+
+            if delta == order_in[0]:
+
+                @pl.when(phase == 1)
+                def _():
+                    push(delta, 1)
 
     for copy in now:
         copy.wait_recv()
@@ -269,12 +280,11 @@
 
     for s in range(4):
         for at, delta in enumerate(order_in):
-            if at == 3 and s < 3:
+            if s < 3 and (at, s) in ((2, 1), (2, 2), (3, 0), (3, 1), (3, 2)):
 
                 @pl.when(phase == s + 1)
                 def _():
-                    push(order_in[0], s + 1)
-                    push(order_in[1], s + 1)
+                    push(order_in[1 if s == 0 else at - 2], s + 1)
 
             wait_chunk(s, delta)
         if s < 3:

time: 197 us -> 192 us (0.975)
  the two profiles are of different devices: /device:TPU:9 before, /device:TPU:25 now
where the time goes in v3:
time: 192 us
  Pallas kernels  188 us (98%)
  other arithmetic  1.97 us (1%)
    pallas_call x1, Pallas kernels, shards(): pl.pallas_call(kernel, out_shape=jax.ShapeDtypeStruct((HELD,) + tile, F32...  188 us

profile of v3, /device:TPU:25, one launch (start us, length us, event | category | flops | bytes accessed | tf_op | source)
XLA Modules:
  0.0 191.7 jit_solution(3731968936073295751)
XLA Ops:
  0.0 2.0 %fusion.8 = (s32[128]{0:T(128)}, s32[128]{0:T(128)}) fusion(s32[256]{0:T(256)S(1)} %get-tuple-element.7, s32[128,256]{1,0:T(8,128)} %param.7, s32[256]{0:T(256)S(1)} %get-tuple-element.8), kind=kLoop, calls=%fused_computation.23 | loop fusion | flops 2227968 | bytes 134144 | tf_op jit(solution)/shard_map/reduce_max | solution.py:41
  2.0 187.8 %shard_map.64 = f32[8,128,128]{2,1,0:T(8,128)} custom-call(s32[128]{0:T(128)} %get-tuple-element.6.row_at, s32[128]{0:T(128)} %get-tuple-element.5.col_at, f32[128]{0:T(128)} %width.1, f32[8,128,128]{2,1,0:T(8,128)} %sky.1, bf16[16,128,2048]{2,1,0:T(8,128)(2,1)} %constant.98.clone.t_hbm, bf16[16,2048,128]{2,1,0:T(8,128)(2,1)} %constant.99.clone.tcol_hbm, ...), custom_call_target="tpu_custom_call" | custom-call | flops 17179869184 | bytes 20971520 | tf_op jit(solution)/shard_map/pallas_call | solution.py:479
  189.8 1.9 copy.8
  (1 shorter events, 0.0 us)

commit v4 on v3

--- a/solution.py
+++ b/solution.py
@@ -246,34 +246,43 @@
 
     sources = [lax.rem(x + 3 - 2 * c, 4) for c in range(2)]
 
-    def row_transform(s):
-        stops = [xrel.at[0, s, c] for c in range(2)]
-
+    def beside(blocks):
+        return blocks[0] if len(blocks) == 1 else jnp.concatenate(blocks, axis=1)
+
+    def row_transform(quarters):
         @pl.loop(0, 4)
         def _(t):
             rel = lax.rem(2 + t + lax.div(t, 2) + 2 * lax.div(t, 3), 4)
             xd = lax.rem(x + rel, 4)
-            slab = jnp.dot(tv[pl.ds(xd * 4, 4)].reshape(SLAB, L), w[s], preferred_element_type=F32)
-            rowsend[s, xd] = slab.astype(BF)
-            deliver(
-                rowsend.at[s, xd], turned.at[x + 4 * s], stops, x_send.at[s], x_recv.at[s], xr_recv.at[0, s], rel, xd
-            )
-
-        homes = [turned.at[source + 4 * s] for source in sources]
-        pass_blocks(stops, homes, xf_send.at[0], x_recv.at[s], xr_recv.at[0, s])
-
-    def add_spectrum(s):
-        wait_bytes(turned.at[4 * s : 4 * s + 4], x_recv.at[s])
-        for k in range(4):
-            a[s, :, k * SIDE : (k + 1) * SIDE] = turned[4 * s + k]
-        places = [lax.rem(4 * s + k + 16 - col_turn, 16) for k in range(4)]
+            slab = jnp.dot(
+                tv[pl.ds(xd * 4, 4)].reshape(SLAB, L), beside([w[s] for s in quarters]), preferred_element_type=F32
+            ).astype(BF)
+            for at, s in enumerate(quarters):
+                stops = [xrel.at[0, s, c] for c in range(2)]
+                rowsend[s, xd] = slab[:, at * SIDE : (at + 1) * SIDE]
+                home = turned.at[x + 4 * s]
+                deliver(rowsend.at[s, xd], home, stops, x_send.at[s], x_recv.at[s], xr_recv.at[0, s], rel, xd)
+
+        for s in quarters:
+            stops = [xrel.at[0, s, c] for c in range(2)]
+            homes = [turned.at[source + 4 * s] for source in sources]
+            pass_blocks(stops, homes, xf_send.at[0], x_recv.at[s], xr_recv.at[0, s])
+
+    def add_spectrum(quarters):
+        places = {}
+        for s in quarters:
+            wait_bytes(turned.at[4 * s : 4 * s + 4], x_recv.at[s])
+            for k in range(4):
+                a[s, :, k * SIDE : (k + 1) * SIDE] = turned[4 * s + k]
+            places[s] = [lax.rem(4 * s + k + 16 - col_turn, 16) for k in range(4)]
         for n in range(4):
             cols = slice(n * SLAB, (n + 1) * SLAB)
-            rhs = jnp.concatenate([tv[j, :, cols] for j in places], axis=0)
-            total = jnp.dot(a[s], rhs, preferred_element_type=F32)
-            if s > 0:
-                total = spec[:, cols] + total
-            if s < 3:
+            total = None if quarters[0] == 0 else spec[:, cols]
+            for s in quarters:
+                rhs = jnp.concatenate([tv[j, :, cols] for j in places[s]], axis=0)
+                term = jnp.dot(a[s], rhs, preferred_element_type=F32)
+                total = term if total is None else total + term
+            if quarters[-1] < 3:
                 spec[:, cols] = total
             else:
                 filt[:, cols] = (trv[:, cols].astype(F32) * total.astype(BF).astype(F32)).astype(BF)
@@ -295,29 +304,37 @@
                 push(order_in[3], s + 1)
 
         weigh(s)
-        row_transform(s)
-        if s > 0:
-            add_spectrum(s - 1)
-    add_spectrum(3)
-
-    def back_transform(s):
-        stops = [xrel.at[1, s, c] for c in range(2)]
-
+        if s == 1:
+            row_transform((0, 1))
+        if s == 2:
+            row_transform((2,))
+            add_spectrum((0, 1))
+        if s == 3:
+            row_transform((3,))
+            add_spectrum((2,))
+    add_spectrum((3,))
+
+    def back_transform(quarters):
         @pl.loop(0, 4)
         def _(t):
             rel = lax.rem(2 + t + lax.div(t, 2) + 2 * lax.div(t, 3), 4)
             xd = lax.rem(x + rel, 4)
-            picked = tcol[lax.rem(xd + 4 * s + 16 - col_turn, 16)]
-            backsend[s, xd] = jnp.dot(filt[...], picked, preferred_element_type=F32).astype(BF)
-            deliver(
-                backsend.at[s, xd], ret.at[s, x], stops, b_send.at[s], b_recv.at[s], xr_recv.at[1, s], rel, xd
-            )
-
-        homes = [ret.at[s, source] for source in sources]
-        pass_blocks(stops, homes, xf_send.at[1], b_recv.at[s], xr_recv.at[1, s])
-
-    def give_back(s):
-        wait_bytes(ret.at[s], b_recv.at[s])
+            picked = beside([tcol[lax.rem(xd + 4 * s + 16 - col_turn, 16)] for s in quarters])
+            back = jnp.dot(filt[...], picked, preferred_element_type=F32).astype(BF)
+            for at, s in enumerate(quarters):
+                stops = [xrel.at[1, s, c] for c in range(2)]
+                backsend[s, xd] = back[:, at * SIDE : (at + 1) * SIDE]
+                home = ret.at[s, x]
+                deliver(backsend.at[s, xd], home, stops, b_send.at[s], b_recv.at[s], xr_recv.at[1, s], rel, xd)
+
+        for s in quarters:
+            stops = [xrel.at[1, s, c] for c in range(2)]
+            homes = [ret.at[s, source] for source in sources]
+            pass_blocks(stops, homes, xf_send.at[1], b_recv.at[s], xr_recv.at[1, s])
+
+    def give_back(quarters):
+        for s in quarters:
+            wait_bytes(ret.at[s], b_recv.at[s])
 
         @pl.loop(0, 4)
         def _(turn):
@@ -325,36 +342,36 @@
             m = lax.rem(z + delta, 4)
             places = [lax.rem(4 * m + yh + 16 - row_turn, 16) for yh in range(4)]
             lhs = jnp.concatenate([tv[i] for i in places], axis=0)
-            smeared = jnp.dot(lhs, ret[s].reshape(L, SIDE), preferred_element_type=F32)
-            for yh in range(4):
-                beam = row_beam[places[yh]] * col_beam[0:1, s * SIDE : (s + 1) * SIDE]
-                tile = smeared[yh * SIDE : (yh + 1) * SIDE]
-                csend[s, delta, yh] = (beam * tile * (1.0 / (L * L))).astype(BF)
+            smeared = jnp.dot(lhs, beside([ret[s].reshape(L, SIDE) for s in quarters]), preferred_element_type=F32)
+            for at, s in enumerate(quarters):
+                for yh in range(4):
+                    beam = row_beam[places[yh]] * col_beam[0:1, s * SIDE : (s + 1) * SIDE]
+                    tile = smeared[yh * SIDE : (yh + 1) * SIDE, at * SIDE : (at + 1) * SIDE]
+                    csend[s, delta, yh] = (beam * tile * (1.0 / (L * L))).astype(BF)
 
             @pl.loop(0, 4)
             def _(step):
                 yh = lax.rem(yhi + step + 2, 4)
-                yd = 2 * yh + s // 2
-                mine = jnp.logical_and(yd == y, core == s % 2)
-                src = csend.at[s, delta, yh]
-                home = grecv.at[delta, me16]
-
-                @pl.when(jnp.logical_not(mine))
-                def _():
-                    remote(src, home, c_send.at[s], c_recv.at[delta], {"y": yd, "core": s % 2}).start()
-
-                @pl.when(mine)
-                def _():
-                    pltpu.make_async_copy(src, home, c_recv.at[delta]).start()
-
-    back_transform(0)
-    back_transform(1)
-    give_back(0)
-    back_transform(2)
-    give_back(1)
-    back_transform(3)
-    give_back(2)
-    give_back(3)
+                for s in quarters:
+                    yd = 2 * yh + s // 2
+                    mine = jnp.logical_and(yd == y, core == s % 2)
+                    src = csend.at[s, delta, yh]
+                    home = grecv.at[delta, me16]
+
+                    @pl.when(jnp.logical_not(mine))
+                    def _():
+                        remote(src, home, c_send.at[s], c_recv.at[delta], {"y": yd, "core": s % 2}).start()
+
+                    @pl.when(mine)
+                    def _():
+                        pltpu.make_async_copy(src, home, c_recv.at[delta]).start()
+
+    back_transform((0,))
+    back_transform((1,))
+    give_back((0,))
+    back_transform((2, 3))
+    give_back((1,))
+    give_back((2, 3))
 
     def add_up(delta):
         wait_bytes(grecv.at[delta], c_recv.at[delta])

time: 192 us -> 195 us (1.016)
  the two profiles are of different devices: /device:TPU:25 before, /device:TPU:9 now
where the time goes in v4:
time: 195 us
  Pallas kernels  191 us (98%)
  other arithmetic  1.97 us (1%)
    pallas_call x1, Pallas kernels, shards(): pl.pallas_call(kernel, out_shape=jax.ShapeDtypeStruct((HELD,) + tile, F32...  191 us

profile of v4, /device:TPU:9, one launch (start us, length us, event | category | flops | bytes accessed | tf_op | source)
XLA Modules:
  0.0 194.6 jit_solution(745732992444007357)
XLA Ops:
  0.0 2.0 %fusion.8 = (s32[128]{0:T(128)}, s32[128]{0:T(128)}) fusion(s32[256]{0:T(256)S(1)} %get-tuple-element.7, s32[128,256]{1,0:T(8,128)} %param.7, s32[256]{0:T(256)S(1)} %get-tuple-element.8), kind=kLoop, calls=%fused_computation.23 | loop fusion | flops 2227968 | bytes 134144 | tf_op jit(solution)/shard_map/reduce_max | solution.py:41
  2.0 190.7 %shard_map.64 = f32[8,128,128]{2,1,0:T(8,128)} custom-call(s32[128]{0:T(128)} %get-tuple-element.6.row_at, s32[128]{0:T(128)} %get-tuple-element.5.col_at, f32[128]{0:T(128)} %width.1, f32[8,128,128]{2,1,0:T(8,128)} %sky.1, bf16[16,128,2048]{2,1,0:T(8,128)(2,1)} %constant.98.clone.t_hbm, bf16[16,2048,128]{2,1,0:T(8,128)(2,1)} %constant.99.clone.tcol_hbm, ...), custom_call_target="tpu_custom_call" | custom-call | flops 17179869184 | bytes 20971520 | tf_op jit(solution)/shard_map/pallas_call | solution.py:496
  192.7 1.9 copy.8
  (1 shorter events, 0.0 us)

commit v5 on v3

--- a/solution.py
+++ b/solution.py
@@ -65,7 +65,7 @@
     pairs = [p0, p1, p2, p3]
     images = [img0, img1, img2, img3]
     order_in = (2, 1, 3, 0)
-    order_out = (0, 1, 3, 2)
+    turns = (0, 2, 1, 3)
 
     def remote(src, dst, s_sem, r_sem, where):
         return pltpu.make_async_remote_copy(
@@ -164,9 +164,9 @@
 
             if delta == order_in[0]:
 
-                @pl.when(phase == 1)
+                @pl.when(phase == turns[1])
                 def _():
-                    push(delta, 1)
+                    push(delta, turns[1])
 
     for copy in now:
         copy.wait_recv()
@@ -278,26 +278,26 @@
             else:
                 filt[:, cols] = (trv[:, cols].astype(F32) * total.astype(BF).astype(F32)).astype(BF)
 
-    for s in range(4):
+    for number, s in enumerate(turns):
+        later = turns[number + 1] if number < 3 else None
         for at, delta in enumerate(order_in):
-            if s < 3 and (at, s) in ((2, 1), (2, 2), (3, 0), (3, 1), (3, 2)):
-
-                @pl.when(phase == s + 1)
+            if later is not None and at > (1 if number == 0 else 0):
+
+                @pl.when(phase == later)
                 def _():
-                    push(order_in[1 if s == 0 else at - 2], s + 1)
+                    push(order_in[at - 1], later)
 
             wait_chunk(s, delta)
-        if s < 3:
-
-            @pl.when(phase == s + 1)
+        if later is not None:
+
+            @pl.when(phase == later)
             def _():
-                push(order_in[2], s + 1)
-                push(order_in[3], s + 1)
+                push(order_in[3], later)
 
         weigh(s)
         row_transform(s)
-        if s > 0:
-            add_spectrum(s - 1)
+        if number > 0:
+            add_spectrum(turns[number - 1])
     add_spectrum(3)
 
     def back_transform(s):
@@ -347,14 +347,14 @@
                 def _():
                     pltpu.make_async_copy(src, home, c_recv.at[delta]).start()
 
-    back_transform(0)
-    back_transform(1)
-    give_back(0)
-    back_transform(2)
-    give_back(1)
-    back_transform(3)
-    give_back(2)
-    give_back(3)
+    back_transform(turns[0])
+    back_transform(turns[1])
+    give_back(turns[0])
+    back_transform(turns[2])
+    give_back(turns[1])
+    back_transform(turns[3])
+    give_back(turns[2])
+    give_back(turns[3])
 
     def add_up(delta):
         wait_bytes(grecv.at[delta], c_recv.at[delta])

time: 192 us -> 174 us (0.906)
  the two profiles are of different devices: /device:TPU:25 before, /device:TPU:9 now
where the time goes in v5:
time: 174 us
  Pallas kernels  170 us (98%)
  other arithmetic  1.97 us (1%)
  local copies, waits for them, and re-layouts  1.87 us (1%)
    pallas_call x1, Pallas kernels, shards(): pl.pallas_call(kernel, out_shape=jax.ShapeDtypeStruct((HELD,) + tile, F32...  170 us

profile of v5, /device:TPU:9, one launch (start us, length us, event | category | flops | bytes accessed | tf_op | source)
XLA Modules:
  0.0 174.3 jit_solution(2428209576005798830)
XLA Ops:
  0.0 2.0 %fusion.8 = (s32[128]{0:T(128)}, s32[128]{0:T(128)}) fusion(s32[256]{0:T(256)S(1)} %get-tuple-element.7, s32[128,256]{1,0:T(8,128)} %param.7, s32[256]{0:T(256)S(1)} %get-tuple-element.8), kind=kLoop, calls=%fused_computation.23 | loop fusion | flops 2227968 | bytes 134144 | tf_op jit(solution)/shard_map/reduce_max | solution.py:41
  2.0 170.4 %shard_map.64 = f32[8,128,128]{2,1,0:T(8,128)} custom-call(s32[128]{0:T(128)} %get-tuple-element.6.row_at, s32[128]{0:T(128)} %get-tuple-element.5.col_at, f32[128]{0:T(128)} %width.1, f32[8,128,128]{2,1,0:T(8,128)} %sky.1, bf16[16,128,2048]{2,1,0:T(8,128)(2,1)} %constant.98.clone.t_hbm, bf16[16,2048,128]{2,1,0:T(8,128)(2,1)} %constant.99.clone.tcol_hbm, ...), custom_call_target="tpu_custom_call" | custom-call | flops 17179869184 | bytes 20971520 | tf_op jit(solution)/shard_map/pallas_call | solution.py:479
  172.4 1.9 %copy.8 = f32[8,128,128]{2,1,0:T(8,128)} copy(f32[8,128,128]{2,1,0:T(8,128)} %shard_map.64) | data formatting | bytes 1048576
  (1 shorter events, 0.0 us)
